TPU v7x, 256 devices: a whole 4x4x8 slice. The times are simulated.
256 devices in a mesh: row: 16 (over z_hi, x), col: 16 (over z_lo, y, core).
Axes of the slice: x: 4, y: 4, z: 8 (z_hi: 4, z_lo: 2; z = z_hi * 2 + z_lo), core: 2. Of those that a mesh axis runs over, the one named last changes fastest.
Arguments:
- hessian: float32 [16, 768, 16, 768], P('row', None, 'col'), may hold values from -6 to 6
- panels: float32 [16, 16, 48, 1024], P('row', 'col'), may hold values from -0.078125 to 0.078125
- factors: float32 [2, 512, 512], replicated, may hold values from -1.6 to 1.6, as said below
Outputs:
- updated: float32 [16, 768, 16, 768], P('row', None, 'col')
Inputs may be any that keep to these rules, and one draw needn't show every extreme that they name: Each of the two factors is upper triangular, with diagonal entries from 0.8 to 1.6.
All inputs are finite; a program needn't handle non-finite values.
Results may differ from a plain program's by a relative error of at most 0.0001.
Values sent between devices are 32-bit elements; how exact they have to be, the bound alone decides.
A program may use at most 128 MiB of HBM per device.

v0:
```python
import jax
import jax.numpy as jnp
from jax import lax
from jax.sharding import PartitionSpec as P

PRECISE = lax.Precision.HIGHEST


def product(left_side, right_side):
    return jnp.dot(left_side, right_side, precision=PRECISE, preferred_element_type=jnp.float32)


def inner_sum(left_side, right_side):
    return lax.dot_general(
        left_side,
        right_side,
        (((0,), (0,)), ((), ())),
        precision=PRECISE,
        preferred_element_type=jnp.float32,
    )


def outer_sum(left_side, right_side):
    return lax.dot_general(
        left_side,
        right_side,
        (((1,), (1,)), ((), ())),
        precision=PRECISE,
        preferred_element_type=jnp.float32,
    )


def apply_matrix(matrix, cols_panel):
    return lax.psum_scatter(product(matrix, cols_panel), "col", scatter_dimension=0, tiled=True)


def finish_factor(basis_piece, image_piece, gram, factor):
    middle = product(factor.T, product(gram, factor))
    return product(image_piece, factor) - 0.5 * product(basis_piece, middle)


def wy_factor(basis_piece, image_piece, factor):
    gram = lax.psum(inner_sum(basis_piece, image_piece), ("row", "col"))
    return finish_factor(basis_piece, image_piece, gram, factor)


def rank_update(matrix, rows_basis, cols_basis, wy_piece):
    wy_rows = lax.all_gather(wy_piece, "col", axis=0, tiled=True)
    wy_cols = lax.all_gather(wy_piece, "row", axis=0, tiled=True)
    return matrix - outer_sum(rows_basis, wy_cols) - outer_sum(wy_rows, cols_basis)


def on_device(hessian, panels, factors):
    row_devices = lax.axis_size("row")
    col_devices = lax.axis_size("col")
    local_tile = hessian[0, :, 0, :]
    tile_span = panels.shape[2]
    panel_width = factors.shape[1]
    quartered = local_tile.reshape(col_devices, tile_span, row_devices, tile_span).transpose(
        0, 3, 2, 1
    )
    mirrored = lax.all_to_all(
        lax.all_to_all(quartered, "row", split_axis=2, concat_axis=2, tiled=True),
        "col",
        split_axis=0,
        concat_axis=0,
        tiled=True,
    )
    symmetric = 0.5 * (local_tile + mirrored.reshape(local_tile.shape))
    basis_piece = panels[0, 0]
    rows_basis = lax.all_gather(basis_piece, "col", axis=0, tiled=True)
    cols_basis = lax.all_gather(basis_piece, "row", axis=0, tiled=True)
    first_basis = basis_piece[:, :panel_width]
    second_basis = basis_piece[:, panel_width:]
    image_one = apply_matrix(symmetric, cols_basis[:, :panel_width])
    wy_one = wy_factor(first_basis, image_one, factors[0])
    stepped = rank_update(
        symmetric, rows_basis[:, :panel_width], cols_basis[:, :panel_width], wy_one
    )
    image_two = apply_matrix(stepped, cols_basis[:, panel_width:])
    wy_two = wy_factor(second_basis, image_two, factors[1])
    updated = rank_update(stepped, rows_basis[:, panel_width:], cols_basis[:, panel_width:], wy_two)
    return updated.reshape(1, updated.shape[0], 1, updated.shape[1])


def solution(mesh):
    return jax.shard_map(
        on_device,
        mesh=mesh,
        in_specs=(P("row", None, "col", None), P("row", "col", None, None), P()),
        out_specs=P("row", None, "col", None),
        check_vma=False,
    )
```

profile of v0, /device:TPU:1, one launch (start us, length us, event | category | flops | bytes accessed | tf_op | source)
XLA Modules:
  0.0 1129.7 jit_solution(8516964888835840793)
XLA Ops:
  6.5 7.3 reduce
  13.8 4.8 reshape_squeeze.3
  18.6 7.4 copy.31
  26.0 8.6 reshape.11
  34.6 11.6 %all-to-all-start = ((f32[16,1,36864]{2,1,0:T(1,128)}), f32[16,1,36864]{2,1,0:T(1,128)S(1)}, u32[]{:S(2)}, u32[]{:S(2)}) async-start(f32[16,1,36864]{2,1,0:T(1,128)} %reshape.11), calls=%async_computation | async-start | bytes 4718592 | tf_op jit(solution)/shard_map/all_to_all | solution.py:63
  46.1 0.5 all-gather.17.cloned.1.call-start
  46.9 56.5 %all-to-all-done = f32[16,1,36864]{2,1,0:T(1,128)S(1)} async-done(((f32[16,1,36864]{2,1,0:T(1,128)}), f32[16,1,36864]{2,1,0:T(1,128)S(1)}, u32[]{:S(2)}, u32[]{:S(2)}) %all-to-all-start) | async-done | bytes 2359328 | tf_op jit(solution)/shard_map/all_to_all | solution.py:63
  103.4 0.6 broadcast.10
  104.0 8.4 reduce.1
  112.3 5.6 reshape.12
  117.9 6.1 copy_bitcast_fusion
  124.0 8.7 reshape.13
  132.6 12.4 %all-to-all-start.1 = ((f32[16,1,36864]{2,1,0:T(1,128)}), f32[16,1,36864]{2,1,0:T(1,128)}, u32[]{:S(2)}, u32[]{:S(2)}) async-start(f32[16,1,36864]{2,1,0:T(1,128)} %reshape.13), calls=%async_computation.1 | async-start | bytes 4718592 | tf_op jit(solution)/shard_map/all_to_all | solution.py:62
  145.2 5.5 copy.20
  150.7 25.2 %all-to-all-done.1 = f32[16,1,36864]{2,1,0:T(1,128)} async-done(((f32[16,1,36864]{2,1,0:T(1,128)}), f32[16,1,36864]{2,1,0:T(1,128)}, u32[]{:S(2)}, u32[]{:S(2)}) %all-to-all-start.1) | async-done | bytes 2359328 | tf_op jit(solution)/shard_map/all_to_all | solution.py:62
  175.9 9.3 reduce.2
  185.2 5.6 reshape.14
  190.8 9.0 copy.23
  199.8 6.2 reshape.6
  206.1 7.3 fusion.12
  213.4 61.5 %reduce-scatter.3.cloned.1.call-done = f32[48,512]{1,0:T(8,128)} async-done(((f32[768,512]{1,0:T(8,128)}), f32[48,512]{1,0:T(8,128)}) %reduce-scatter.3.cloned.1.call-update) | async-done | bytes 98320 | tf_op jit(solution)/shard_map/reduce_scatter | solution.py:34
  274.9 2.9 convolution_bitcast_fusion.1
  277.9 0.5 all-gather.19.cloned.1.call-update
  278.5 258.5 %all-reduce.3.cloned.1.call-done = f32[512,512]{0,1:T(8,128)} async-done(((f32[512,512]{0,1:T(8,128)}), f32[512,512]{0,1:T(8,128)}) %all-reduce.3.cloned.1.call-update) | async-done | bytes 1048592 | tf_op jit(solution)/shard_map/psum | solution.py:43
  537.0 3.1 fusion.23
  540.1 1.8 fusion.21
  542.0 1.1 fusion.15
  543.1 1.4 convolution_subtract_fusion.1
  544.5 0.5 all-gather.11.cloned.1.call-update
  545.0 0.4 reduce-scatter.5.cloned.1.call-start
  545.5 32.1 %all-gather.19.cloned.1.call-done = f32[1,1,768,1024]{3,2,1,0:T(8,128)} async-done(((f32[1,1,48,1024]{3,2,1,0:T(8,128)}), f32[1,1,768,1024]{3,2,1,0:T(8,128)}) %all-gather.19.cloned.1.call-update) | async-done | bytes 3145744 | tf_op jit(solution)/shard_map/all_gather | solution.py:71
  577.6 56.3 %all-gather.9.cloned.1.call-done = f32[768,512]{1,0:T(8,128)} async-done(((f32[48,512]{1,0:T(8,128)}), f32[768,512]{1,0:T(8,128)}) %all-gather.9.cloned.1.call-update) | async-done | bytes 1572880 | tf_op jit(solution)/shard_map/all_gather | solution.py:49
  633.9 7.3 fusion.6
  641.2 30.1 %all-gather.11.cloned.1.call-done = f32[768,512]{1,0:T(8,128)} async-done(((f32[48,512]{1,0:T(8,128)}), f32[768,512]{1,0:T(8,128)}) %all-gather.11.cloned.1.call-update) | async-done | bytes 1572880 | tf_op jit(solution)/shard_map/all_gather | solution.py:48
  671.3 8.2 fusion.2
  679.5 5.2 fusion.9
  684.8 61.4 %reduce-scatter.5.cloned.1.call-done = f32[48,512]{1,0:T(8,128)} async-done(((f32[768,512]{1,0:T(8,128)}), f32[48,512]{1,0:T(8,128)}) %reduce-scatter.5.cloned.1.call-update) | async-done | bytes 98320 | tf_op jit(solution)/shard_map/reduce_scatter | solution.py:34
  746.2 2.9 convolution_bitcast_fusion
  749.1 258.9 %all-reduce.5.cloned.1.call-done = f32[512,512]{0,1:T(8,128)} async-done(((f32[512,512]{0,1:T(8,128)}), f32[512,512]{0,1:T(8,128)}) %all-reduce.5.cloned.1.call-update) | async-done | bytes 1048592 | tf_op jit(solution)/shard_map/psum | solution.py:43
  1008.0 3.5 fusion.18
  1011.6 1.8 fusion.16
  1013.4 1.1 fusion.14
  1014.6 1.4 convolution_subtract_fusion
  1016.6 54.0 %all-gather.13.cloned.1.call-done = f32[768,512]{1,0:T(8,128)} async-done(((f32[48,512]{1,0:T(8,128)}), f32[768,512]{1,0:T(8,128)}) %all-gather.13.cloned.1.call-update) | async-done | bytes 1572880 | tf_op jit(solution)/shard_map/all_gather | solution.py:49
  1070.5 7.2 fusion.4
  1077.8 30.1 %all-gather.15.cloned.1.call-done = f32[768,512]{1,0:T(8,128)} async-done(((f32[48,512]{1,0:T(8,128)}), f32[768,512]{1,0:T(8,128)}) %all-gather.15.cloned.1.call-update) | async-done | bytes 1572880 | tf_op jit(solution)/shard_map/all_gather | solution.py:48
  1107.9 8.2 fusion.1
  1116.0 6.6 copy.26
  (33 shorter events, 1.4 us)
Async XLA Ops:
  34.6 68.8 %all-to-all-start = ((f32[16,1,36864]{2,1,0:T(1,128)}), f32[16,1,36864]{2,1,0:T(1,128)S(1)}, u32[]{:S(2)}, u32[]{:S(2)}) async-start(f32[16,1,36864]{2,1,0:T(1,128)} %reshape.11), calls=%async_computation | async-start | bytes 4718592 | tf_op jit(solution)/shard_map/all_to_all | solution.py:63
  46.1 159.9 %all-gather.17.cloned.1.call-start = ((), (), s32[]{:S(2)}) async-start(), calls=%async_computation.12 | async-start | bytes 3342336 | tf_op jit(solution)/shard_map/all_gather | solution.py:72
  132.6 43.3 %all-to-all-start.1 = ((f32[16,1,36864]{2,1,0:T(1,128)}), f32[16,1,36864]{2,1,0:T(1,128)}, u32[]{:S(2)}, u32[]{:S(2)}) async-start(f32[16,1,36864]{2,1,0:T(1,128)} %reshape.13), calls=%async_computation.1 | async-start | bytes 4718592 | tf_op jit(solution)/shard_map/all_to_all | solution.py:62
  145.0 129.9 %reduce-scatter.3.cloned.1.call-start = ((), (), s32[]{:S(2)}) async-start(), calls=%async_computation.4 | async-start | bytes 1671168 | tf_op jit(solution)/shard_map/reduce_scatter | solution.py:34
  150.7 55.4 %copy-start = (f32[1,768,1,768]{1,3,2,0:T(8,128)}, f32[1,768,1,768]{1,3,2,0:T(8,128)S(1)}, u32[]{:S(2)}) copy-start(f32[1,768,1,768]{1,3,2,0:T(8,128)S(1)} %copy.20) | copy-start | bytes 7077892
  206.1 68.8 %copy-start.4 = (f32[1,1,48,1024]{3,2,1,0:T(8,128)S(1)}, f32[1,1,48,1024]{3,2,1,0:T(8,128)}, u32[]{:S(2)}) copy-start(f32[1,1,48,1024]{3,2,1,0:T(8,128)} %param.4) | copy-start | bytes 589828
  213.4 323.6 %copy-start.1 = (f32[2,512,512]{2,1,0:T(8,128)S(1)}, f32[2,512,512]{2,1,0:T(8,128)}, u32[]{:S(2)}) copy-start(f32[2,512,512]{2,1,0:T(8,128)} %param.5) | copy-start | bytes 6291460
  213.4 323.6 %all-reduce.3.cloned.1.call-start = ((), (), s32[]{:S(2)}) async-start(), calls=%async_computation.5 | async-start | bytes 2097152 | tf_op jit(solution)/shard_map/psum | solution.py:43
  277.8 299.8 %all-gather.19.cloned.1.call-start = ((), (), s32[]{:S(2)}) async-start(), calls=%async_computation.13 | async-start | bytes 3342336 | tf_op jit(solution)/shard_map/all_gather | solution.py:71
  278.4 355.5 %all-gather.9.cloned.1.call-start = ((), (), s32[]{:S(2)}) async-start(), calls=%async_computation.6 | async-start | bytes 1671168 | tf_op jit(solution)/shard_map/all_gather | solution.py:49
  540.1 1.9 copy-start.5
  540.1 3.0 copy-start.6
  544.5 126.8 %all-gather.11.cloned.1.call-start = ((), (), s32[]{:S(2)}) async-start(), calls=%async_computation.7 | async-start | bytes 1671168 | tf_op jit(solution)/shard_map/all_gather | solution.py:48
  545.0 201.1 %reduce-scatter.5.cloned.1.call-start = ((), (), s32[]{:S(2)}) async-start(), calls=%async_computation.8 | async-start | bytes 1671168 | tf_op jit(solution)/shard_map/reduce_scatter | solution.py:34
  671.3 8.2 copy-start.3
  684.7 323.3 %all-reduce.5.cloned.1.call-start = ((), (), s32[]{:S(2)}) async-start(), calls=%async_computation.9 | async-start | bytes 2097152 | tf_op jit(solution)/shard_map/psum | solution.py:43
  749.1 321.4 %all-gather.13.cloned.1.call-start = ((), (), s32[]{:S(2)}) async-start(), calls=%async_computation.10 | async-start | bytes 1671168 | tf_op jit(solution)/shard_map/all_gather | solution.py:49
  1008.0 3.5 copy-start.2
  1011.6 3.0 copy-start.7
  1016.0 91.9 %all-gather.15.cloned.1.call-start = ((), (), s32[]{:S(2)}) async-start(), calls=%async_computation.11 | async-start | bytes 1671168 | tf_op jit(solution)/shard_map/all_gather | solution.py:48
Sparse Core Ops, SparseCore 0:
  49.4 89.2 all-gather.16
  213.5 61.3 reduce-scatter.2
  281.2 255.6 all-reduce.2
  538.7 38.9 all-gather.18
  579.9 53.9 all-gather.8
  635.6 35.5 all-gather.10
  684.8 61.2 reduce-scatter.4
  752.5 255.4 all-reduce.4
  1016.1 54.3 all-gather.12
  1072.2 35.5 all-gather.14
where the time goes:
time: 1140 us; the launch traced here: 1130 us
  waiting for transfers between devices  926 us (81%)
  local copies, waits for them, and re-layouts  74.6 us (7%)
  matrix products  64.4 us (6%)
  starting transfers between devices  25.6 us (2%)
  other arithmetic  25 us (2%)
  between operations  14 us (1%)
    psum x2, waiting for transfers between devices, wy_factor(): gram = lax.psum(inner_sum(basis_piece, image_piece), ('row', 'col'))  517 us
    reduce_scatter x2, waiting for transfers between devices, apply_matrix(): lax.psum_scatter(product(matrix, cols_panel), 'col', scatter_dimension=0,...  123 us
    all_gather x2, waiting for transfers between devices, rank_update(): wy_cols = lax.all_gather(wy_piece, 'row', axis=0, tiled=True)  110 us
    all_gather x2, waiting for transfers between devices, rank_update(): wy_rows = lax.all_gather(wy_piece, 'col', axis=0, tiled=True)  60.1 us
    all_to_all x1, waiting for transfers between devices, on_device(): lax.all_to_all(quartered, 'row', split_axis=2, concat_axis=2, tiled=True)  56.5 us
    unnamed x22, local copies, waits for them, and re-layouts  39.9 us
    all_gather x1, waiting for transfers between devices, on_device(): rows_basis = lax.all_gather(basis_piece, 'col', axis=0, tiled=True)  32.1 us
    dot_general x4, matrix products, outer_sum(): lax.dot_general(left_side, right_side, (((1,), (1,)), ((), ())), precisio...  30.9 us
  transfers between devices with their start and end apart: 12, of which 11 were waited for; matrix products, arithmetic and copies ran while one was open for 8% of the time, Pallas kernels for 0%

commit v1 on v0

v1 whole, which is shorter than its diff:
```python
import functools

import jax
import jax.numpy as jnp
from jax import lax
from jax.experimental import pallas as pl
from jax.experimental.pallas import tpu as pltpu
from jax.sharding import PartitionSpec as P

MESH = pl.DeviceIdType.MESH
F32, BF16 = jnp.float32, jnp.bfloat16
NX, NY, NZ = 4, 4, 8
W = 48
M = 768
B = 512
U = 2 * B


def split(value):
    high = value.astype(BF16)
    return high, (value - high.astype(F32)).astype(BF16)


def put(ref, where, value):
    high, low = split(value)
    ref[(0,) + where] = high
    ref[(1,) + where] = low


def mm(left, right, dims=((1,), (0,))):
    def one(a, b):
        return lax.dot_general(a, b, (dims, ((), ())), preferred_element_type=F32)

    return one(left[0], right[0]) + (one(left[0], right[1]) + one(left[1], right[0]))


NT = ((1,), (1,))


def hl(ref, *where):
    return ref[(0,) + where], ref[(1,) + where]


class Place:
    def __init__(self):
        row, col = lax.axis_index("row"), lax.axis_index("col")
        self.zh, self.x = row // NX, row % NX
        self.zl, self.y, self.k = col // (2 * NY), (col // 2) % NY, col % 2
        self.z = self.zh * 2 + self.zl
        self.f = row
        self.slot = self.slot_of(self.k, self.zl, self.y)

    def slot_of(self, k, zl, y):
        return k * 8 + zl * 4 + y

    def at(self, dx=0, dy=0, dz=0, dk=0):
        x, y, z = (self.x + dx) % NX, (self.y + dy) % NY, (self.z + dz) % NZ
        k = (self.k + dk) % 2
        return {"row": (z // 2) * NX + x, "col": (z % 2) * 2 * NY + y * 2 + k}

    def zl_peer(self):
        return {"col": (1 - self.zl) * 2 * NY + self.y * 2 + self.k, "row": self.f}


class Mail:
    def __init__(self, send_sems, recv_sems):
        self.send_sems, self.recv_sems, self.sent = send_sems, recv_sems, []

    def send(self, src, dst, target):
        index = len(self.sent)
        copy = pltpu.make_async_remote_copy(
            src, dst, self.send_sems.at[index], self.recv_sems.at[index], device_id=target, device_id_type=MESH
        )
        copy.start()
        self.sent.append(copy)
        return copy

    def close(self):
        for copy in self.sent:
            copy.wait_send()


def greet(partners):
    barrier = pltpu.get_barrier_semaphore()
    for target in partners:
        pl.semaphore_signal(barrier, inc=1, device_id=target, device_id_type=MESH)
    pl.semaphore_wait(barrier, len(partners))


def rows48(slot):
    return pl.ds(pl.multiple_of(slot * W, 8), W)


def gather_row(mail, here, buf):
    def block(zh, x):
        return buf.at[rows48(zh * NX + x)]

    mine = block(here.zh, here.x)
    far = [mail.send(mine, mine, here.at(dz=2 * d)) for d in (1, 2, 3)]
    last = [mail.send(mine, mine, here.at(dx=d)) for d in (1, 2, 3)]
    yield
    for d in (1, 2, 3):
        far[d - 1].wait_recv()
        got = block((here.zh + 4 - d) % 4, here.x)
        last += [mail.send(got, got, here.at(dx=e)) for e in (1, 2, 3)]
        yield
    for copy in last:
        copy.wait_recv()
    yield


def gather_col(mail, here, buf):
    def block(zl):
        return buf.at[rows48(here.slot_of(here.k, zl, here.y))]

    mine = block(here.zl)
    pair = mail.send(mine, mine, here.zl_peer())
    first = [mail.send(mine, mine, here.at(dy=d)) for d in (1, 2, 3)]
    yield
    pair.wait_recv()
    got = block(1 - here.zl)
    second = [mail.send(got, got, here.at(dy=d)) for d in (1, 2, 3)]
    yield
    last = []
    for zl, copies in ((here.zl, first), (1 - here.zl, second)):
        for copy in copies:
            copy.wait_recv()
        part = buf.at[pl.ds(pl.multiple_of((here.k * 8 + zl * 4) * W, 8), 4 * W)]
        last.append(mail.send(part, part, here.at(dk=1)))
        yield
    for copy in last:
        copy.wait_recv()
    yield


def all_reduce(mail, here, part, out, from_k, from_x, from_y, from_z):
    q = from_z.shape[0] // 7
    block = 8 * q

    def rows(start, count):
        return pl.ds(pl.multiple_of(start, 8), count)

    def add(start, ref, count, pieces):
        where = rows(start, count)
        total = part[where, :]
        for p in range(pieces):
            total = total + ref[p * count : (p + 1) * count, :]
        return where, total

    half, plane = 16 * block, 4 * block
    copy = mail.send(part.at[rows((1 - here.k) * half, half)], from_k, here.at(dk=1))
    yield
    copy.wait_recv()
    base = here.k * half

    @pl.loop(0, 4)
    def _(i):
        where = rows(base + i * plane, plane)
        part[where, :] = part[where, :] + from_k[rows(i * plane, plane), :]

    copies = [
        mail.send(
            part.at[rows(base + (here.x + d) % 4 * plane, plane)],
            from_x.at[pl.ds((d - 1) * plane, plane)],
            here.at(dx=d),
        )
        for d in (1, 2, 3)
    ]
    yield
    for copy in copies:
        copy.wait_recv()
    base = base + here.x * plane
    where, total = add(base, from_x, plane, 3)
    part[where, :] = total
    copies = [
        mail.send(
            part.at[rows(base + (here.y + d) % 4 * block, block)],
            from_y.at[pl.ds((d - 1) * block, block)],
            here.at(dy=d),
        )
        for d in (1, 2, 3)
    ]
    yield
    for copy in copies:
        copy.wait_recv()
    base = base + here.y * block
    where, total = add(base, from_y, block, 3)
    part[where, :] = total
    copies = [
        mail.send(
            part.at[rows(base + (here.z + d) % 8 * q, q)], from_z.at[pl.ds((d - 1) * q, q)], here.at(dz=d)
        )
        for d in range(1, 8)
    ]
    yield
    for copy in copies:
        copy.wait_recv()
    _, total = add(base + here.z * q, from_z, q, 7)
    base = ((here.k * 4 + here.y) * 4 + here.x) * block
    mine = rows(base + here.z * q, q)
    out[mine, :] = total
    copies = [mail.send(out.at[mine], out.at[mine], here.at(dz=d)) for d in range(1, 8)]
    yield
    for copy in copies:
        copy.wait_recv()
    mine = out.at[rows(base, block)]
    copies = [mail.send(mine, mine, here.at(dx=d)) for d in (1, 2, 3)]
    yield
    for copy in copies:
        copy.wait_recv()
    mine = out.at[rows((here.k * 4 + here.y) * plane, plane)]
    copies = [mail.send(mine, mine, here.at(dy=d)) for d in (1, 2, 3)]
    yield
    for copy in copies:
        copy.wait_recv()
    mine = out.at[rows(here.k * half, half)]
    copy = mail.send(mine, mine, here.at(dk=1))
    yield
    copy.wait_recv()
    yield


def square(ref, block, which):
    parts = []
    for j in range(4):
        start, stop = (which * 4 + j) * B, (which * 4 + j + 1) * B
        pieces = []
        while start < stop:
            index = start // block
            end = min(stop, (index + 1) * block)
            k, x, y = index // 16, index // 4 % 4, index % 4
            at = (k * 16 + y * 4 + x) * block + start - index * block
            pieces.append(ref[at : at + end - start, :])
            start = end
        parts.append(jnp.concatenate(pieces, axis=0))
    return jnp.concatenate(parts, axis=1)


def mirror_kernel(
    h, u, t,
    s_out, sh_out, uch_out, urh_out, tch_out, trt_out, bch_out, brh_out, eh_out,
    lt, bz, bx, bs, m, uc, ur, th, eh,
    sh, uch, urh, tch, trt, bch, brh,
    e_part, e_out, e_k, e_x, e_y, e_z,
    send_sems, recv_sems, local_sems,
):
    here = Place()
    greet(
        [here.at(dx=d) for d in (1, 2, 3)]
        + [here.at(dz=d) for d in range(1, 8)]
        + [here.at(dy=d, dk=e) for d in range(4) for e in range(2) if d or e]
    )
    mail = Mail(send_sems, recv_sems)
    uc[rows48(here.f), :] = u[...]
    ur[rows48(here.slot), :] = u[...]
    row_steps, col_steps = gather_row(mail, here, uc), gather_col(mail, here, ur)
    next(row_steps)
    next(col_steps)

    for zl in range(2):
        for j in range(6):
            lt[zl, 128 * j : 128 * j + 128, :] = h[pl.ds(zl * 384 * 6 + j, 384, stride=6), :].T
    z_copies = []
    for d in range(1, 8):
        z = (here.z + d) % 8
        block = lt.at[z % 2, pl.ds(pl.multiple_of(z // 2 * 192, 8), 192)]
        z_copies.append(mail.send(block, bz.at[here.z], here.at(dz=d)))
    bz[here.z] = lt[here.zl, pl.ds(pl.multiple_of(here.zh * 192, 8), 192), :]

    for p in range(2):
        high, low = split(t[p])
        th[0, p], th[1, p] = high, low
    own_second = split(mm(split(u[:, B:]), (th[0, 1], th[1, 1])))
    part = mm(split(u[:, :B].T), own_second)
    for j in range(4):
        e_part[j * B : (j + 1) * B, :] = part[:, 128 * j : 128 * j + 128]
    e_steps = all_reduce(mail, here, e_part, e_out, e_k, e_x, e_y, e_z)
    next(e_steps)

    x_copies = {}

    def along_x(d):
        z = (here.z + 8 - d) % 8
        x_copies[d] = []
        for e in (1, 2, 3):
            x_copies[d].append(
                mail.send(bz.at[z, rows48((here.x + e) % 4)], bx.at[here.x, z], here.at(dx=e))
            )
        bx[here.x, z] = bz[z, rows48(here.x), :]

    def shuffle(zl):
        for i in range(8):
            pieces = [
                bx[x, zh * 2 + zl, :, i * W : (i + 1) * W] for zh in range(4) for x in range(4)
            ]
            bs[i % 2 * 4 + i // 2, zl] = jnp.concatenate(pieces, axis=1)
        copies = []
        for dk in range(2):
            for dy in range(4):
                source = bs.at[(here.k + dk) % 2 * 4 + (here.y + dy) % 4, zl]
                where = rows48(here.slot_of(here.k, zl, here.y))
                if dk or dy:
                    copies.append(mail.send(source, m.at[where], here.at(dy=dy, dk=dk)))
                else:
                    m[where, :] = source[...]
        return copies

    along_x(0)
    next(e_steps)
    next(row_steps)
    next(col_steps)
    next(e_steps)
    next(row_steps)
    next(e_steps)
    next(row_steps)
    next(e_steps)
    for d in (2, 6, 4):
        z_copies[d - 1].wait_recv()
        along_x(d)
    for _ in range(2):
        next(e_steps)
        next(col_steps)
    for d in (0, 2, 6, 4):
        for copy in x_copies[d]:
            copy.wait_recv()
    m_copies = shuffle(here.zl)
    next(e_steps)
    for d in (1, 7):
        z_copies[d - 1].wait_recv()
        along_x(d)
    next(e_steps)
    for d in (3, 5):
        z_copies[d - 1].wait_recv()
        along_x(d)
    for d in (1, 7, 3, 5):
        for copy in x_copies[d]:
            copy.wait_recv()
    m_copies += shuffle(1 - here.zl)
    next(row_steps)
    next(col_steps)

    e = square(e_out, 64, 0)
    put(eh, (0,), e)
    put(eh, (1,), e.T)

    def bases(src, uh, bh, turned):
        @pl.loop(0, 3)
        def _(i):
            rows = pl.ds(pl.multiple_of(i * 256, 256), 256)
            value = src[rows, :]
            first, second = split(value[:, :B]), split(value[:, B:])
            for p in range(2):
                uh[p, rows, :B] = first[p]
                uh[p, rows, B:] = second[p]
            put(bh, (rows, slice(None)), value[:, :B] - mm(second, (eh[0, 0], eh[1, 0]), NT))
            for p, half in ((0, first), (1, second)):
                turned(rows, p, mm(half, (th[0, p], th[1, p])))

    def as_is(rows, p, value):
        put(tch, (rows, slice(p * B, p * B + B)), value)

    def transposed(rows, p, value):
        put(trt, (slice(p * B, p * B + B), rows), value.T)

    bases(uc, uch, bch, as_is)
    bases(ur, urh, brh, transposed)
    leaving = []

    def leave(src, dst):
        copy = pltpu.make_async_copy(src, dst, local_sems.at[len(leaving)])
        copy.start()
        leaving.append(copy)

    for src, dst in (
        (uch, uch_out), (urh, urh_out), (tch, tch_out), (trt, trt_out),
        (bch, bch_out), (brh, brh_out), (eh, eh_out),
    ):
        leave(src, dst)
    for copy in m_copies:
        copy.wait_recv()

    @pl.loop(0, 16)
    def _(slot):
        tile_row = slot // 4 % 2 * 8 + slot % 4 * 2 + slot // 8
        rows = rows48(slot)
        for j in range(6):
            cols = slice(128 * j, 128 * j + 128)
            value = 0.5 * (h[pl.ds(tile_row * (6 * W) + j, W, stride=6), :] + m[rows, cols])
            m[rows, cols] = value
            put(sh, (rows, cols), value)

    leave(sh, sh_out)
    leave(m, s_out)
    for copy in leaving:
        copy.wait()
    mail.close()


def panels_kernel(
    s_in, sh_in, uch_in, urh_in, tch_in, trt_in, bch_in, brh_in, eh_in,
    out,
    s, sh, uch, urh, tch, trt, bch, brh, eh,
    xf, xh, r1, r2, r3, xc, xr, udh, dh,
    k_part, k_out, k_k, k_x, k_y, k_z,
    send_sems, recv_sems, local_sems,
):
    here = Place()
    coming = {}
    for name, src, dst in (
        ("sh", sh_in, sh), ("tch", tch_in, tch), ("trt", trt_in, trt), ("eh", eh_in, eh),
        ("urh", urh_in, urh), ("uch", uch_in, uch), ("s", s_in, s), ("bch", bch_in, bch), ("brh", brh_in, brh),
    ):
        coming[name] = pltpu.make_async_copy(src, dst, local_sems.at[len(coming)])
        coming[name].start()
    greet(
        [here.at(dx=d) for d in (1, 2, 3)]
        + [here.at(dy=d) for d in (1, 2, 3)]
        + [here.at(dz=d) for d in range(1, 8)]
        + [here.at(dk=1)]
    )
    mail = Mail(send_sems, recv_sems)
    coming["sh"].wait()
    coming["tch"].wait()

    def image(k):
        rows = pl.ds(pl.multiple_of(k * 384, 128), 384)

        @pl.loop(0, 4)
        def _(j):
            cols = pl.ds(pl.multiple_of(j * 256, 256), 256)
            value = mm(hl(sh, rows, slice(None)), hl(tch, slice(None), cols))
            xf[rows, cols] = value
            put(xh, (rows, cols), value)

        return xf.at[rows]

    x_core = mail.send(image(1 - here.k), r1, here.at(dk=1))
    image(here.k)
    x_core.wait_recv()

    @pl.loop(0, 8)
    def _(i):
        r1[rows48(i), :] = r1[rows48(i), :] + xf[rows48(here.k * 8 + i), :]

    x_y = []
    for d in (1, 2, 3):
        for zl in range(2):
            x_y.append(
                mail.send(r1.at[rows48(zl * 4 + (here.y + d) % 4)], r2.at[d - 1, zl], here.at(dy=d))
            )

    coming["trt"].wait()

    @pl.loop(0, 6)
    def _(i):
        which = i // 2
        left = pl.ds(pl.multiple_of(which // 2 * B, B), B)
        cols = pl.ds(pl.multiple_of((which + 1) // 2 * B + i % 2 * 256, 256), 256)
        value = mm(hl(trt, left, slice(None)), hl(xh, slice(None), cols))
        for j in range(2):
            k_part[pl.ds(pl.multiple_of((i * 2 + j) * B, B), B), :] = value[:, 128 * j : 128 * j + 128]

    k_steps = all_reduce(mail, here, k_part, k_out, k_k, k_x, k_y, k_z)
    next(k_steps)
    next(k_steps)
    for copy in x_y:
        copy.wait_recv()
    for zl in range(2):
        where = rows48(zl * 4 + here.y)
        r1[where, :] = r1[where, :] + (r2[0, zl] + r2[1, zl] + r2[2, zl])
    x_z = mail.send(r1.at[rows48((1 - here.zl) * 4 + here.y)], r3, here.zl_peer())
    next(k_steps)
    x_z.wait_recv()
    piece = r1[rows48(here.zl * 4 + here.y), :] + r3[...]
    xc[rows48(here.f), :] = piece
    xr[rows48(here.slot), :] = piece
    row_steps, col_steps = gather_row(mail, here, xc), gather_col(mail, here, xr)
    next(row_steps)
    next(col_steps)
    next(k_steps)
    next(k_steps)
    next(col_steps)
    next(k_steps)
    next(row_steps)
    next(k_steps)
    next(row_steps)
    next(row_steps)
    next(col_steps)
    next(col_steps)
    next(k_steps)
    next(k_steps)

    for name in ("eh", "urh", "uch", "s"):
        coming[name].wait()
    z1 = square(k_out, 192, 0)
    k12 = square(k_out, 192, 1)
    z1e = mm(split(z1), (eh[0, 0], eh[1, 0]))
    turned = mm((eh[0, 1], eh[1, 1]), split(k12 - 0.5 * z1e))
    z2 = square(k_out, 192, 2) - (turned + turned.T)
    corner = z1e - k12
    put(dh, (slice(0, B), slice(0, B)), -z1)
    put(dh, (slice(0, B), slice(B, U)), corner)
    put(dh, (slice(B, U), slice(0, B)), corner.T)
    put(dh, (slice(B, U), slice(B, U)), -z2)

    @pl.loop(0, 4)
    def _(j):
        cols = pl.ds(pl.multiple_of(j * 256, 256), 256)
        put(udh, (slice(None), cols), mm(hl(urh, slice(None), slice(None)), hl(dh, slice(None), cols)))

    @pl.loop(0, 3)
    def _(j):
        cols = pl.ds(pl.multiple_of(j * 256, 256), 256)
        s[:, cols] = s[:, cols] - mm(hl(udh, slice(None), slice(None)), hl(uch, cols, slice(None)), NT)

    coming["bch"].wait()
    coming["brh"].wait()
    next(col_steps)
    next(row_steps)

    @pl.loop(0, 3)
    def _(i):
        rows = pl.ds(pl.multiple_of(i * 256, 256), 256)
        put(xh, (rows, slice(None)), xr[rows, :])
        put(tch, (rows, slice(None)), xc[rows, :])

    one, two, every = slice(0, B), slice(B, U), slice(None)

    @pl.loop(0, 3)
    def _(j):
        cols = pl.ds(pl.multiple_of(j * 256, 256), 256)
        value = s[:, cols] - mm(hl(xh, every, one), hl(bch, cols, every), NT)
        value = value - mm(hl(xh, every, two), hl(uch, cols, two), NT)
        value = value - mm(hl(brh, every, every), hl(tch, cols, one), NT)
        value = value - mm(hl(urh, every, two), hl(tch, cols, two), NT)
        for slot in range(16):
            tile_row = slot // 4 % 2 * 8 + slot % 4 * 2 + slot // 8
            for e in range(2):
                where = pl.ds(tile_row * (6 * W) + j * 2 + e, W, stride=6)
                out[where, :] = value[slot * W : (slot + 1) * W, 128 * e : 128 * e + 128]

    mail.close()


def vmem(*shape, dtype=F32):
    return pltpu.VMEM(shape, dtype)


def on_device(hessian, panels, factors):
    tile = hessian.reshape(M * 6, 128)
    piece = panels.reshape(W, U)
    in_vmem, anywhere = pl.BlockSpec(memory_space=pltpu.VMEM), pl.BlockSpec(memory_space=pl.ANY)
    shapes = [
        ((M, M), F32), ((2, M, M), BF16), ((2, M, U), BF16), ((2, M, U), BF16), ((2, M, U), BF16),
        ((2, U, M), BF16), ((2, M, B), BF16), ((2, M, B), BF16), ((2, 2, B, B), BF16),
    ]
    sums = lambda q: [vmem(256 * q, 128), vmem(128 * q, 128), vmem(96 * q, 128), vmem(24 * q, 128), vmem(7 * q, 128)]
    sems = pltpu.SemaphoreType.DMA
    middle = pl.pallas_call(
        mirror_kernel,
        name="mirror",
        out_shape=[jax.ShapeDtypeStruct(*shape) for shape in shapes],
        in_specs=[in_vmem] * 3,
        out_specs=[anywhere] * 9,
        scratch_shapes=[
            vmem(2, M, 384), vmem(8, 192, 384), vmem(4, 8, W, 384), vmem(8, 2, W, M), vmem(M, M),
            vmem(M, U), vmem(M, U), vmem(2, 2, B, B, dtype=BF16), vmem(2, 2, B, B, dtype=BF16),
            *[vmem(*shape, dtype=dtype) for shape, dtype in shapes[1:8]],
            vmem(2048, 128), *sums(8),
            sems((104,)), sems((104,)), sems((9,)),
        ],
        compiler_params=pltpu.CompilerParams(
            collective_id=0, has_side_effects=True, vmem_limit_bytes=60 << 20
        ),
    )(tile, piece, factors)
    updated = pl.pallas_call(
        panels_kernel,
        name="panels",
        out_shape=jax.ShapeDtypeStruct((M * 6, 128), F32),
        in_specs=[anywhere] * 9,
        out_specs=in_vmem,
        scratch_shapes=[
            *[vmem(*shape, dtype=dtype) for shape, dtype in shapes],
            vmem(M, U), vmem(2, M, U, dtype=BF16), vmem(M // 2, U), vmem(3, 2, W, U), vmem(W, U),
            vmem(M, U), vmem(M, U), vmem(2, M, U, dtype=BF16), vmem(2, U, U, dtype=BF16),
            vmem(6144, 128), *sums(24),
            sems((72,)), sems((72,)), sems((9,)),
        ],
        compiler_params=pltpu.CompilerParams(
            collective_id=1, has_side_effects=True, vmem_limit_bytes=62 << 20
        ),
    )(*middle)
    return updated.reshape(1, M, 1, M)


def solution(mesh):
    return jax.shard_map(
        on_device,
        mesh=mesh,
        in_specs=(P("row", None, "col", None), P("row", "col", None, None), P()),
        out_specs=P("row", None, "col", None),
        check_vma=False,
    )
```

time: 1140 us -> 266 us (0.23)
  waiting for transfers between devices: 926 us -> 0 us
  Pallas kernels: 0 us -> 262 us
  local copies, waits for them, and re-layouts: 74.6 us -> 4.69 us
  matrix products: 64.4 us -> 0 us
  starting transfers between devices: 25.6 us -> 0 us
  other arithmetic: 25 us -> 0 us
  between operations: 14 us -> 0.02 us
    psum x2 -> x0, waiting for transfers between devices: 517 us -> none  [wy_factor(): gram = lax.psum(inner_sum(basis_piece, image_piece), ('row', 'col'))]
    pallas_call x0 -> x2, Pallas kernels: none -> 262 us  [the longest x1 141 us: on_device(): pl.pallas_call(mirror_kernel, name='mirror', out_shape=[jax.ShapeDtypeStr...]
    all_gather x6 -> x0, waiting for transfers between devices: 203 us -> none  [the longest x2 110 us: rank_update(): wy_cols = lax.all_gather(wy_piece, 'row', axis=0, tiled=True)]
    reduce_scatter x2 -> x0, waiting for transfers between devices: 123 us -> none  [apply_matrix(): lax.psum_scatter(product(matrix, cols_panel), 'col', scatter_dimension=0,...]
    all_to_all x2 -> x0, waiting for transfers between devices: 81.7 us -> none  [the longest x1 56.5 us: on_device(): lax.all_to_all(quartered, 'row', split_axis=2, concat_axis=2, tiled=True)]
    dot_general x16 -> x0, matrix products: 64.4 us -> none  [the longest x4 30.9 us: outer_sum(): lax.dot_general(left_side, right_side, (((1,), (1,)), ((), ())), precisio...]
    unnamed x22 -> x1, local copies, waits for them, and re-layouts: 39.9 us -> 4.69 us
    all_to_all x2 -> x0, starting transfers between devices: 23.9 us -> none  [the longest x1 12.4 us: on_device(): lax.all_to_all(lax.all_to_all(quartered, 'row', split_axis=2, concat_axis...]
  transfers between devices with their start and end apart: 12 -> 0, of which waited for: 11 -> 0; matrix products, arithmetic and copies ran while one was open for 8% -> 0% of each run, Pallas kernels for 0% -> 0%
where the time goes in v1:
time: 266 us
  Pallas kernels  262 us (98%)
  local copies, waits for them, and re-layouts  4.69 us (2%)
    pallas_call x1, Pallas kernels, on_device(): pl.pallas_call(mirror_kernel, name='mirror', out_shape=[jax.ShapeDtypeStr...  141 us
    pallas_call x1, Pallas kernels, on_device(): pl.pallas_call(panels_kernel, name='panels', out_shape=jax.ShapeDtypeStru...  120 us

profile of v1, /device:TPU:1, one launch (start us, length us, event | category | flops | bytes accessed | tf_op | source)
XLA Modules:
  0.0 266.3 jit_solution(3593879038385361658)
XLA Ops:
  0.0 141.2 %mirror.1 = (f32[768,768]{1,0:T(8,128)}, bf16[2,768,768]{2,1,0:T(8,128)(2,1)}, bf16[2,768,1024]{2,1,0:T(8,128)(2,1)}, bf16[2,768,1024]{2,1,0:T(8,128)(2,1)}, bf1...) custom-call(f32[4608,128]{1,0:T(8,128)} %bitcast.4, ...), custom_call_target="tpu_custom_call" | custom-call | tf_op jit(solution)/shard_map/mirror/pallas_call | solution.py:559
  141.2 120.4 %panels.1 = f32[4608,128]{1,0:T(8,128)} custom-call(f32[768,768]{1,0:T(8,128)} %get-tuple-element.14.s_in, bf16[2,768,768]{2,1,0:T(8,128)(2,1)} %get-tuple-element.15.sh_in, bf16[2,768,1024]{2,1,0:T(8,128)(2,1)} %get-tuple-element.16.uch_in, bf16[2,768,1024]{2,1,0:T(8,128)(2,1)} %get-tuple-element.17.urh_in, bf16[2,768,1024]{2,1,0:T(8,128)(2,1)} %get-tuple-element.18.tch_in, ...), custom_call_target="tpu_custom_call" | custom-call | tf_op jit(solution)/shard_map/panels/pallas_call | solution.py:576
  261.6 4.7 %copy.6 = f32[1,768,1,768]{3,2,1,0:T(1,128)} copy(f32[1,768,1,768]{3,2,1,0:T(1,128)} %bitcast.3) | data formatting | bytes 4718592

commit v2 on v0

v2 whole, which is shorter than its diff:
```python
import jax
import jax.numpy as jnp
from jax import lax
from jax.experimental import pallas as pl
from jax.experimental.pallas import tpu as pltpu
from jax.sharding import PartitionSpec as P

MESH = pl.DeviceIdType.MESH
F32, BF16 = jnp.float32, jnp.bfloat16
NX, NY, NZ = 4, 4, 8
W = 48
M = 768
B = 512
U = 2 * B


def split(value):
    high = value.astype(BF16)
    return high, (value - high.astype(F32)).astype(BF16)


def put(ref, where, value):
    high, low = split(value)
    ref[(0,) + where] = high
    ref[(1,) + where] = low


def mm(left, right, dims=((1,), (0,))):
    def one(a, b):
        return lax.dot_general(a, b, (dims, ((), ())), preferred_element_type=F32)

    return one(left[0], right[0]) + (one(left[0], right[1]) + one(left[1], right[0]))


NT = ((1,), (1,))


def hl(ref, *where):
    return ref[(0,) + where], ref[(1,) + where]


class Place:
    def __init__(self):
        row, col = lax.axis_index("row"), lax.axis_index("col")
        self.zh, self.x = row // NX, row % NX
        self.zl, self.y, self.k = col // (2 * NY), (col // 2) % NY, col % 2
        self.z = self.zh * 2 + self.zl
        self.f = row
        self.slot = self.slot_of(self.k, self.zl, self.y)

    def slot_of(self, k, zl, y):
        return k * 8 + zl * 4 + y

    def at(self, dx=0, dy=0, dz=0, dk=0):
        x, y, z = (self.x + dx) % NX, (self.y + dy) % NY, (self.z + dz) % NZ
        k = (self.k + dk) % 2
        return {"row": (z // 2) * NX + x, "col": (z % 2) * 2 * NY + y * 2 + k}

    def zl_peer(self):
        return {"col": (1 - self.zl) * 2 * NY + self.y * 2 + self.k, "row": self.f}


class Mail:
    def __init__(self, send_sems, recv_sems):
        self.send_sems, self.recv_sems, self.open, self.count = send_sems, recv_sems, [], 0

    def send(self, src, dst, target):
        index = self.count
        self.count += 1
        copy = pltpu.make_async_remote_copy(
            src, dst, self.send_sems.at[index], self.recv_sems.at[index], device_id=target, device_id_type=MESH
        )
        copy.start()
        self.open.append(copy)
        return copy

    def settle(self, copies=None):
        leaving = list(self.open if copies is None else copies)
        for copy in leaving:
            copy.wait_send()
        self.open = [copy for copy in self.open if not any(copy is other for other in leaving)]


def greet(partners):
    barrier = pltpu.get_barrier_semaphore()
    for target in partners:
        pl.semaphore_signal(barrier, inc=1, device_id=target, device_id_type=MESH)
    pl.semaphore_wait(barrier, len(partners))


def rows48(slot):
    return pl.ds(pl.multiple_of(slot * W, 8), W)


def logged(mail, log):
    def send(*args):
        log.append(mail.send(*args))
        return log[-1]

    return send


def gather_row(mail, here, buf, log):
    send = logged(mail, log)

    def block(zh, x):
        return buf.at[rows48(zh * NX + x)]

    mine = block(here.zh, here.x)
    far = [send(mine, mine, here.at(dz=2 * d)) for d in (1, 2, 3)]
    last = [send(mine, mine, here.at(dx=d)) for d in (1, 2, 3)]
    yield
    for d in (1, 2, 3):
        far[d - 1].wait_recv()
        got = block((here.zh + 4 - d) % 4, here.x)
        last += [send(got, got, here.at(dx=e)) for e in (1, 2, 3)]
        yield
    for copy in last:
        copy.wait_recv()
    yield


def gather_col(mail, here, buf, log):
    send = logged(mail, log)

    def block(zl):
        return buf.at[rows48(here.slot_of(here.k, zl, here.y))]

    mine = block(here.zl)
    pair = send(mine, mine, here.zl_peer())
    first = [send(mine, mine, here.at(dy=d)) for d in (1, 2, 3)]
    yield
    pair.wait_recv()
    got = block(1 - here.zl)
    second = [send(got, got, here.at(dy=d)) for d in (1, 2, 3)]
    yield
    last = []
    for zl, copies in ((here.zl, first), (1 - here.zl, second)):
        for copy in copies:
            copy.wait_recv()
        part = buf.at[pl.ds(pl.multiple_of((here.k * 8 + zl * 4) * W, 8), 4 * W)]
        last.append(send(part, part, here.at(dk=1)))
        yield
    for copy in last:
        copy.wait_recv()
    yield


def all_reduce(mail, here, part, out, from_k, from_y, from_x, from_z, swap):
    half = part.shape[0] // 2
    plane, block = half // 4, half // 16

    def rows(start, count):
        return pl.ds(pl.multiple_of(start, 8), count)

    def lanes(z):
        return pl.ds(pl.multiple_of(z * 128, 128), 128)

    def add(where, ref, count):
        total = part[where, :]
        for p in range(3):
            total = total + ref[p * count : (p + 1) * count, :]
        part[where, :] = total

    copy = mail.send(part.at[rows((1 - here.k) * half, half)], from_k, here.at(dk=1))
    yield
    copy.wait_recv()
    base = here.k * half

    @pl.loop(0, 4)
    def _(i):
        where = rows(base + i * plane, plane)
        part[where, :] = part[where, :] + from_k[rows(i * plane, plane), :]

    copies = [
        mail.send(
            part.at[rows(base + (here.y + d) % 4 * plane, plane)],
            from_y.at[pl.ds((d - 1) * plane, plane)],
            here.at(dy=d),
        )
        for d in (1, 2, 3)
    ]
    yield
    for copy in copies:
        copy.wait_recv()
    base = base + here.y * plane
    add(rows(base, plane), from_y, plane)
    copies = [
        mail.send(
            part.at[rows(base + (here.x + d) % 4 * block, block)],
            from_x.at[pl.ds((d - 1) * block, block)],
            here.at(dx=d),
        )
        for d in (1, 2, 3)
    ]
    yield
    for copy in copies:
        copy.wait_recv()
    where = rows(base + here.x * block, block)
    add(where, from_x, block)
    copies = [
        mail.send(
            part.at[where, lanes((here.z + d) % 8)], from_z.at[pl.ds((d - 1) * block, block)], here.at(dz=d)
        )
        for d in range(1, 8)
    ]
    yield
    for copy in copies:
        copy.wait_recv()
    total = part[where, lanes(here.z)]
    for p in range(7):
        total = total + from_z[p * block : (p + 1) * block, :]
    outer, inner = (here.x, here.y) if swap else (here.y, here.x)
    base = (here.k * 4 + outer) * plane
    where = rows(base + inner * block, block)
    out[where, lanes(here.z)] = total
    mine = out.at[where, lanes(here.z)]
    copies = [mail.send(mine, mine, here.at(dz=d)) for d in range(1, 8)]
    yield
    for copy in copies:
        copy.wait_recv()
    mine = out.at[where]
    copies = [mail.send(mine, mine, here.at(dy=d) if swap else here.at(dx=d)) for d in (1, 2, 3)]
    yield
    for copy in copies:
        copy.wait_recv()
    mine = out.at[rows(base, plane)]
    copies = [mail.send(mine, mine, here.at(dx=d) if swap else here.at(dy=d)) for d in (1, 2, 3)]
    yield
    for copy in copies:
        copy.wait_recv()
    mine = out.at[rows(here.k * half, half)]
    copy = mail.send(mine, mine, here.at(dk=1))
    yield
    copy.wait_recv()
    yield


def columns(j):
    return pl.ds(pl.multiple_of(j * 256, 256), 256)


EVERY, ONE, TWO = slice(None), slice(0, B), slice(B, U)


def kernel(
    h, u, t, out,
    hb, lt, bz, bx, m, uc, ur, th,
    uch, urh, p0, p1, p2, bch, brh,
    e_part, e_out, e_k, e_y, e_x, e_z,
    xt, q1, q2, r1, r2, r3,
    k_part, k_out, k_k, k_y, k_x, k_z,
    send_sems, recv_sems, local_sems,
):
    here = Place()
    loads = [
        pltpu.make_async_copy(t.at[0], xt.at[pl.ds(0, B), pl.ds(0, B)], local_sems.at[0]),
        pltpu.make_async_copy(t.at[1], xt.at[pl.ds(0, B), pl.ds(B, B)], local_sems.at[1]),
        pltpu.make_async_copy(h, hb, local_sems.at[2]),
    ]
    for copy in loads:
        copy.start()
    greet(
        [here.at(dx=d) for d in (1, 2, 3)]
        + [here.at(dz=d) for d in range(1, 8)]
        + [here.at(dy=d, dk=e) for d in range(4) for e in range(2) if d or e]
    )
    mail = Mail(send_sems, recv_sems)
    uc[rows48(here.f), :] = u[...]
    ur[rows48(here.slot), :] = u[...]
    row_log, col_log = [], []
    row_steps, col_steps = gather_row(mail, here, uc, row_log), gather_col(mail, here, ur, col_log)
    next(row_steps)
    next(col_steps)

    loads[0].wait()
    loads[1].wait()
    for p in range(2):
        high, low = split(xt[:B, p * B : p * B + B])
        th[0, p], th[1, p] = high, low
    own_second = split(mm(split(u[:, B:]), (th[0, 1], th[1, 1])))
    part = mm(split(u[:, :B].T), own_second)
    e_part[:, :B] = part[:256]
    e_part[:, B:] = part[256:]
    e_steps = all_reduce(mail, here, e_part, e_out, e_k, e_y, e_x, e_z, False)
    next(e_steps)
    next(col_steps)

    loads[2].wait()
    for zl in range(2):
        for j in range(6):
            pieces = [
                hb[pl.ds((zl * 8 + y * 2 + k) * 6 * W + j, W, stride=6), :] for k in range(2) for y in range(4)
            ]
            lt[zl, 128 * j : 128 * j + 128, :] = jnp.concatenate(pieces, axis=0).T
    next(e_steps)
    next(row_steps)
    next(row_steps)
    next(row_steps)
    z_copies = []
    for d in (2, 6, 4, 1, 7, 3, 5):
        z = (here.z + d) % 8
        block = lt.at[z % 2, pl.ds(pl.multiple_of(z // 2 * 192, 8), 192)]
        z_copies.append((d, mail.send(block, bz.at[here.z], here.at(dz=d))))
    z_copies = dict(z_copies)
    bz[here.z] = lt[here.zl, pl.ds(pl.multiple_of(here.zh * 192, 8), 192), :]
    next(e_steps)
    next(col_steps)
    next(e_steps)
    next(col_steps)
    next(e_steps)
    next(col_steps)

    def bases(src, uh, turned):
        @pl.loop(0, 3)
        def _(i):
            rows = columns(i)
            for p in range(2):
                half = split(src[rows, p * B : p * B + B])
                uh[0, rows, p * B : p * B + B] = half[0]
                uh[1, rows, p * B : p * B + B] = half[1]
                turned(rows, p, mm(half, (th[0, p], th[1, p])))

    def row_side(rows, p, value):
        put(p0, (rows, slice(p * B, p * B + B)), value)
        put(p2, (slice(p * B, p * B + B), rows), value.T)

    def col_side(rows, p, value):
        put(p1, (rows, slice(p * B, p * B + B)), value)

    bases(ur, urh, row_side)

    @pl.loop(0, 2)
    def _(i):
        rows = pl.ds(pl.multiple_of(i * 384, 128), 384)
        pieces = [lt[zl, rows, k * 192 : k * 192 + 192] for k in range(2) for zl in range(2)]
        put(p1, (slice(0, 384), slice(0, M)), jnp.concatenate(pieces, axis=1))

        @pl.loop(0, 4)
        def _(j):
            xt[rows, columns(j)] = mm(hl(p1, slice(0, 384), slice(0, M)), hl(p0, EVERY, columns(j)))

    mail.settle(col_log)
    t_x = []
    for e in (1, 2, 3):
        for zh in range(4):
            t_x.append(mail.send(xt.at[rows48(zh * 4 + (here.x + e) % 4)], q1.at[e - 1, zh], here.at(dx=e)))
    next(e_steps)
    next(row_steps)
    bases(uc, uch, col_side)
    mail.settle(row_log)

    def image(k):
        rows = pl.ds(pl.multiple_of(k * 384, 128), 384)
        for zl in range(2):
            for y in range(4):
                for j in range(6):
                    start = (zl * 8 + y * 2 + k) * 6 * W + j
                    at = (zl * 4 + y) * W
                    put(p0, (slice(at, at + W), slice(128 * j, 128 * j + 128)), hb[pl.ds(start, W, stride=6), :])

        @pl.loop(0, 4)
        def _(j):
            uc[rows, columns(j)] = mm(hl(p0, slice(0, 384), slice(0, M)), hl(p1, EVERY, columns(j)))

        return uc.at[rows]

    x_core = mail.send(image(1 - here.k), r1, here.at(dk=1))
    image(here.k)

    for j in range(4):
        right = split(uc[:, 256 * j : 256 * j + 256])
        c = j % 2
        where = slice(B + 256 * c, B + 256 * c + 256)
        value = mm(hl(p2, ONE, EVERY), right)
        if j < 2:
            k_part[:B, 256 * c : 256 * c + 256] = value
        else:
            k_part[:B, where] = k_part[:B, where] + 0.5 * value
        value = mm(hl(p2, TWO, EVERY), right)
        if j < 2:
            k_part[256 * c : 256 * c + 256, B:] = 0.5 * value.T
        else:
            k_part[B:, 256 * c : 256 * c + 256] = value[:256]
            k_part[B:, where] = value[256:]
    k_steps = all_reduce(mail, here, k_part, k_out, k_k, k_y, k_x, k_z, True)
    next(k_steps)
    x_core.wait_recv()
    mail.settle([x_core])

    @pl.loop(0, 8)
    def _(i):
        r1[rows48(i), :] = r1[rows48(i), :] + uc[rows48(here.k * 8 + i), :]

    x_y = []
    for d in (1, 2, 3):
        for zl in range(2):
            x_y.append(
                mail.send(r1.at[rows48(zl * 4 + (here.y + d) % 4)], r2.at[d - 1, zl], here.at(dy=d))
            )
    next(k_steps)
    next(e_steps)
    next(e_steps)
    next(e_steps)

    x_copies = {}

    def along_x(d):
        z = (here.z + 8 - d) % 8
        x_copies[d] = []
        for e in (1, 2, 3):
            x_copies[d].append(
                mail.send(bz.at[z, rows48((here.x + e) % 4)], bx.at[here.x, z], here.at(dx=e))
            )
        bx[here.x, z] = bz[z, rows48(here.x), :]

    def shuffle(zl):
        for i in range(8):
            for half in range(2):
                pieces = [
                    bx[x, (half * 2 + zh) * 2 + zl, :, i * W : (i + 1) * W] for zh in range(2) for x in range(4)
                ]
                lt[half, rows48(zl * 8 + i), :] = jnp.concatenate(pieces, axis=1)
        copies = []
        where = rows48(here.slot_of(here.k, zl, here.y))
        for dk in range(2):
            for dy in range(4):
                rows = rows48(zl * 8 + (here.k + dk) % 2 * 4 + (here.y + dy) % 4)
                if dk or dy:
                    copies.append(mail.send(lt.at[:, rows], m.at[:, where], here.at(dy=dy, dk=dk)))
                else:
                    m[:, where, :] = lt[:, rows, :]
        return copies

    e = jnp.concatenate([e_out[:, :B], e_out[:, B:]], axis=0)
    for p, value in ((0, e), (1, e.T)):
        high, low = split(value)
        th[0, p], th[1, p] = high, low

    def less(uh, bh):
        @pl.loop(0, 3)
        def _(i):
            rows = columns(i)
            first = uh[0, rows, ONE].astype(F32) + uh[1, rows, ONE].astype(F32)
            put(bh, (rows, EVERY), first - mm(hl(uh, rows, TWO), (th[0, 0], th[1, 0]), NT))

    less(uch, bch)
    less(urh, brh)

    along_x(0)
    for d in (2, 6, 4):
        z_copies[d].wait_recv()
        along_x(d)
    for copy in t_x:
        copy.wait_recv()
    for zh in range(4):
        where = rows48(zh * 4 + here.x)
        xt[where, :] = xt[where, :] + (q1[0, zh] + q1[1, zh] + q1[2, zh])
    t_z = [
        mail.send(xt.at[rows48((here.zh + d) % 4 * 4 + here.x)], q2.at[d - 1], here.at(dz=2 * d))
        for d in (1, 2, 3)
    ]
    for copy in x_y:
        copy.wait_recv()
    for zl in range(2):
        where = rows48(zl * 4 + here.y)
        r1[where, :] = r1[where, :] + (r2[0, zl] + r2[1, zl] + r2[2, zl])
    x_z = mail.send(r1.at[rows48((1 - here.zl) * 4 + here.y)], r3, here.zl_peer())
    next(k_steps)
    for d in (1, 7, 3, 5):
        z_copies[d].wait_recv()
        along_x(d)
    mail.settle(z_copies.values())
    for d in (0, 2, 6, 4):
        for copy in x_copies[d]:
            copy.wait_recv()
    m_copies = shuffle(here.zl)
    next(k_steps)
    x_z.wait_recv()
    for copy in t_z:
        copy.wait_recv()
    piece = r1[rows48(here.zl * 4 + here.y), :] + r3[...]
    piece = 0.5 * (piece + xt[rows48(here.f), :] + (q2[0] + q2[1] + q2[2]))
    xr, xc = uc, ur
    xc[rows48(here.f), :] = piece
    xr[rows48(here.slot), :] = piece
    row_steps, col_steps = gather_row(mail, here, xc, []), gather_col(mail, here, xr, [])
    next(row_steps)
    next(col_steps)
    next(k_steps)
    next(k_steps)
    next(col_steps)
    next(k_steps)
    next(row_steps)
    next(row_steps)
    next(row_steps)
    for d in (1, 7, 3, 5):
        for copy in x_copies[d]:
            copy.wait_recv()
    m_copies += shuffle(1 - here.zl)
    next(col_steps)
    next(col_steps)
    next(k_steps)
    next(k_steps)
    mail.settle()

    @pl.loop(0, 32)
    def _(i):
        k, y, x = i // 16, i // 4 % 4, i % 4
        k_part[pl.ds(pl.multiple_of(i * 24, 8), 24), :] = k_out[
            pl.ds(pl.multiple_of((k * 16 + x * 4 + y) * 24, 8), 24), :
        ]

    k_part[:B, :B] = 0.5 * (k_part[:B, :B] + k_part[:B, :B].T)

    @pl.loop(0, 2)
    def _(c):
        cols, right = columns(c), columns(c + 2)
        z1e = mm(split(k_part[:B, :B]), (th[0, 0, :, cols], th[1, 0, :, cols]))
        k12 = k_part[:B, right]
        xt[:B, right] = z1e - k12
        turned = mm((th[0, 1], th[1, 1]), split(k12 - 0.5 * z1e))
        k_part[B:, cols] = 0.5 * k_part[B:, cols] - turned[:256]
        k_part[B:, right] = 0.5 * k_part[B:, right] - turned[256:]

    xt[:B, :B] = -k_part[:B, :B]
    for c, ref, rows in ((0, xt, slice(B, M)), (1, e_part, slice(0, 256))):
        cols, right = slice(256 * c, 256 * c + 256), slice(B + 256 * c, B + 256 * c + 256)
        ref[rows, :B] = xt[:B, right].T
        turned = jnp.concatenate([k_part[B:, cols].T, k_part[B:, right].T], axis=1)
        ref[rows, B:] = -(k_part[B:, B * c : B * c + B] + turned)
    for i in range(4):
        rows = xt[256 * i : 256 * i + 256, :] if i < 3 else e_part[...]
        put(p2, (slice(256 * i, 256 * i + 256), EVERY), mm(split(rows), hl(uch, EVERY, EVERY), NT))

    def add_to_tile(j, scale, value):
        for slot in range(16):
            tile_row = slot // 4 % 2 * 8 + slot % 4 * 2 + slot // 8
            for e in range(2):
                where = pl.ds(tile_row * (6 * W) + j * 2 + e, W, stride=6)
                hb[where, :] = scale * hb[where, :] - value[slot * W : (slot + 1) * W, 128 * e : 128 * e + 128]

    @pl.loop(0, 3)
    def _(j):
        add_to_tile(j, 0.5, mm(hl(urh, EVERY, EVERY), hl(p2, EVERY, columns(j))))

    next(col_steps)
    next(row_steps)

    @pl.loop(0, 3)
    def _(i):
        put(p0, (columns(i), EVERY), xr[columns(i), :])
        put(p1, (columns(i), EVERY), xc[columns(i), :])

    @pl.loop(0, 3)
    def _(j):
        rows = columns(j)
        value = mm(hl(p0, EVERY, ONE), hl(bch, rows, EVERY), NT)
        value = value + mm(hl(p0, EVERY, TWO), hl(uch, rows, TWO), NT)
        value = value + mm(hl(brh, EVERY, EVERY), hl(p1, rows, ONE), NT)
        value = value + mm(hl(urh, EVERY, TWO), hl(p1, rows, TWO), NT)
        add_to_tile(j, 1.0, value)

    for copy in m_copies:
        copy.wait_recv()

    @pl.loop(0, 16)
    def _(slot):
        tile_row = slot // 4 % 2 * 8 + slot % 4 * 2 + slot // 8
        for j in range(6):
            where = pl.ds(tile_row * (6 * W) + j, W, stride=6)
            hb[where, :] = hb[where, :] + 0.5 * m[j // 3, rows48(slot), 128 * (j % 3) : 128 * (j % 3) + 128]

    mail.settle()
    last = pltpu.make_async_copy(hb, out, local_sems.at[3])
    last.start()
    last.wait()


def vmem(*shape, dtype=F32):
    return pltpu.VMEM(shape, dtype)


def on_device(hessian, panels, factors):
    anywhere = pl.BlockSpec(memory_space=pl.ANY)

    def sums(rows):
        return [vmem(rows, U), vmem(rows, U), vmem(rows // 2, U), vmem(rows * 3 // 8, U),
                vmem(rows * 3 // 32, U), vmem(rows * 7 // 32, 128)]

    updated = pl.pallas_call(
        kernel,
        name="panels",
        out_shape=jax.ShapeDtypeStruct((M * 6, 128), F32),
        in_specs=[anywhere, pl.BlockSpec(memory_space=pltpu.VMEM), anywhere],
        out_specs=anywhere,
        scratch_shapes=[
            vmem(M * 6, 128), vmem(2, M, 384), vmem(8, 192, 384), vmem(4, 8, W, 384), vmem(2, M, 384),
            vmem(M, U), vmem(M, U), vmem(2, 2, B, B, dtype=BF16),
            *[vmem(2, M, U, dtype=BF16)] * 4, vmem(2, U, M, dtype=BF16), *[vmem(2, M, B, dtype=BF16)] * 2,
            *sums(256),
            vmem(M, U), vmem(3, 4, W, U), vmem(3, W, U), vmem(M // 2, U), vmem(3, 2, W, U), vmem(W, U),
            *sums(M),
            pltpu.SemaphoreType.DMA((176,)), pltpu.SemaphoreType.DMA((176,)), pltpu.SemaphoreType.DMA((4,)),
        ],
        compiler_params=pltpu.CompilerParams(
            collective_id=0, has_side_effects=True, vmem_limit_bytes=63 << 20
        ),
    )(hessian.reshape(M * 6, 128), panels.reshape(W, U), factors)
    return updated.reshape(1, M, 1, M)


def solution(mesh):
    return jax.shard_map(
        on_device,
        mesh=mesh,
        in_specs=(P("row", None, "col", None), P("row", "col", None, None), P()),
        out_specs=P("row", None, "col", None),
        check_vma=False,
    )
```

time: 1140 us -> 290 us (0.25)
  waiting for transfers between devices: 926 us -> 0 us
  Pallas kernels: 0 us -> 280 us
  local copies, waits for them, and re-layouts: 74.6 us -> 4.69 us
  matrix products: 64.4 us -> 0 us
  starting transfers between devices: 25.6 us -> 0 us
  other arithmetic: 25 us -> 0 us
  between operations: 14 us -> 0.01 us
    psum x2 -> x0, waiting for transfers between devices: 517 us -> none  [wy_factor(): gram = lax.psum(inner_sum(basis_piece, image_piece), ('row', 'col'))]
    pallas_call x0 -> x1, Pallas kernels: none -> 280 us  [on_device(): pl.pallas_call(kernel, name='panels', out_shape=jax.ShapeDtypeStruct((M *...]
    all_gather x6 -> x0, waiting for transfers between devices: 203 us -> none  [the longest x2 110 us: rank_update(): wy_cols = lax.all_gather(wy_piece, 'row', axis=0, tiled=True)]
    reduce_scatter x2 -> x0, waiting for transfers between devices: 123 us -> none  [apply_matrix(): lax.psum_scatter(product(matrix, cols_panel), 'col', scatter_dimension=0,...]
    all_to_all x2 -> x0, waiting for transfers between devices: 81.7 us -> none  [the longest x1 56.5 us: on_device(): lax.all_to_all(quartered, 'row', split_axis=2, concat_axis=2, tiled=True)]
    dot_general x16 -> x0, matrix products: 64.4 us -> none  [the longest x4 30.9 us: outer_sum(): lax.dot_general(left_side, right_side, (((1,), (1,)), ((), ())), precisio...]
    unnamed x22 -> x1, local copies, waits for them, and re-layouts: 39.9 us -> 4.69 us
    all_to_all x2 -> x0, starting transfers between devices: 23.9 us -> none  [the longest x1 12.4 us: on_device(): lax.all_to_all(lax.all_to_all(quartered, 'row', split_axis=2, concat_axis...]
  transfers between devices with their start and end apart: 12 -> 0, of which waited for: 11 -> 0; matrix products, arithmetic and copies ran while one was open for 8% -> 0% of each run, Pallas kernels for 0% -> 0%
where the time goes in v2:
time: 290 us; the launch traced here: 284 us
  Pallas kernels  280 us (97%)
  local copies, waits for them, and re-layouts  4.69 us (2%)
    pallas_call x1, Pallas kernels, on_device(): pl.pallas_call(kernel, name='panels', out_shape=jax.ShapeDtypeStruct((M *...  280 us

profile of v2, /device:TPU:1, one launch (start us, length us, event | category | flops | bytes accessed | tf_op | source)
XLA Modules:
  0.0 284.3 jit_solution(17261895476097942270)
XLA Ops:
  0.0 279.6 %panels.1 = f32[4608,128]{1,0:T(8,128)} custom-call(f32[4608,128]{1,0:T(8,128)} %bitcast.4, f32[48,1024]{1,0:T(8,128)} %bitcast.5, f32[2,512,512]{2,1,0:T(8,128)} %t.1), custom_call_target="tpu_custom_call" | custom-call | tf_op jit(solution)/shard_map/panels/pallas_call | solution.py:591
  279.6 4.7 %copy.6 = f32[1,768,1,768]{3,2,1,0:T(1,128)} copy(f32[1,768,1,768]{3,2,1,0:T(1,128)} %bitcast.3) | data formatting | bytes 4718592

commit v3 on v2

--- a/solution.py
+++ b/solution.py
@@ -102,20 +102,41 @@
 
 def gather_row(mail, here, buf, log):
     send = logged(mail, log)
+    halves = []
 
     def block(zh, x):
-        return buf.at[rows48(zh * NX + x)]
+        return buf.at[rows48(zh % 4 * NX + x % NX)]
+
+    def half(zh, x, which):
+        return buf.at[rows48(zh % 4 * NX + x % NX), pl.ds(which * B, B)]
+
+    def both(zh):
+        mine = block(zh, here.x)
+        return zh, send(mine, mine, here.at(dx=1)), send(mine, mine, here.at(dx=3))
+
+    def pass_on(zh, from_left, from_right):
+        from_left.wait_recv()
+        part = half(zh, here.x + 3, 0)
+        halves.append(send(part, part, here.at(dx=1)))
+        from_right.wait_recv()
+        part = half(zh, here.x + 1, 1)
+        halves.append(send(part, part, here.at(dx=3)))
 
     mine = block(here.zh, here.x)
-    far = [send(mine, mine, here.at(dz=2 * d)) for d in (1, 2, 3)]
-    last = [send(mine, mine, here.at(dx=d)) for d in (1, 2, 3)]
-    yield
-    for d in (1, 2, 3):
-        far[d - 1].wait_recv()
-        got = block((here.zh + 4 - d) % 4, here.x)
-        last += [send(got, got, here.at(dx=e)) for e in (1, 2, 3)]
+    far = {d: send(mine, mine, here.at(dz=2 * d)) for d in (1, 3)}
+    group = both(here.zh)
+    yield
+    for d in (1, 3, 2):
+        far[d].wait_recv()
+        if d == 1:
+            far[2] = send(mine, mine, here.at(dz=4))
+        later = both(here.zh + 4 - d)
+        pass_on(*group)
+        group = later
         yield
-    for copy in last:
+    pass_on(*group)
+    yield
+    for copy in halves:
         copy.wait_recv()
     yield
 
@@ -248,7 +269,7 @@
     hb, lt, bz, bx, m, uc, ur, th,
     uch, urh, p0, p1, p2, bch, brh,
     e_part, e_out, e_k, e_y, e_x, e_z,
-    xt, q1, q2, r1, r2, r3,
+    xt, q0, q1, q2, r1, r2, r3,
     k_part, k_out, k_k, k_y, k_x, k_z,
     send_sems, recv_sems, local_sems,
 ):
@@ -293,20 +314,17 @@
                 hb[pl.ds((zl * 8 + y * 2 + k) * 6 * W + j, W, stride=6), :] for k in range(2) for y in range(4)
             ]
             lt[zl, 128 * j : 128 * j + 128, :] = jnp.concatenate(pieces, axis=0).T
-    next(e_steps)
-    next(row_steps)
-    next(row_steps)
-    next(row_steps)
-    z_copies = []
+    next(row_steps)
+    next(row_steps)
+    next(row_steps)
+    z_copies = {}
     for d in (2, 6, 4, 1, 7, 3, 5):
         z = (here.z + d) % 8
         block = lt.at[z % 2, pl.ds(pl.multiple_of(z // 2 * 192, 8), 192)]
-        z_copies.append((d, mail.send(block, bz.at[here.z], here.at(dz=d))))
-    z_copies = dict(z_copies)
+        z_copies[d] = mail.send(block, bz.at[here.z], here.at(dz=d))
     bz[here.z] = lt[here.zl, pl.ds(pl.multiple_of(here.zh * 192, 8), 192), :]
-    next(e_steps)
-    next(col_steps)
-    next(e_steps)
+    next(col_steps)
+    next(row_steps)
     next(col_steps)
     next(e_steps)
     next(col_steps)
@@ -341,14 +359,25 @@
             xt[rows, columns(j)] = mm(hl(p1, slice(0, 384), slice(0, M)), hl(p0, EVERY, columns(j)))
 
     mail.settle(col_log)
-    t_x = []
-    for e in (1, 2, 3):
-        for zh in range(4):
-            t_x.append(mail.send(xt.at[rows48(zh * 4 + (here.x + e) % 4)], q1.at[e - 1, zh], here.at(dx=e)))
-    next(e_steps)
+
+    def target(zh, dx):
+        return rows48(zh * 4 + (here.x + dx) % 4)
+
+    t_half = []
+    for zh in range(4):
+        t_half.append(mail.send(xt.at[target(zh, 2), pl.ds(0, B)], q0.at[0, zh], here.at(dx=1)))
+        t_half.append(mail.send(xt.at[target(zh, 2), pl.ds(B, B)], q0.at[1, zh], here.at(dx=3)))
     next(row_steps)
     bases(uc, uch, col_side)
     mail.settle(row_log)
+    for copy in t_half:
+        copy.wait_recv()
+    t_x = []
+    for zh in range(4):
+        xt[target(zh, 1), ONE] = xt[target(zh, 1), ONE] + q0[0, zh]
+        xt[target(zh, 3), TWO] = xt[target(zh, 3), TWO] + q0[1, zh]
+        t_x.append(mail.send(xt.at[target(zh, 1)], q1.at[0, zh], here.at(dx=1)))
+        t_x.append(mail.send(xt.at[target(zh, 3)], q1.at[1, zh], here.at(dx=3)))
 
     def image(k):
         rows = pl.ds(pl.multiple_of(k * 384, 128), 384)
@@ -383,10 +412,10 @@
         else:
             k_part[B:, 256 * c : 256 * c + 256] = value[:256]
             k_part[B:, where] = value[256:]
+    mail.settle([x_core])
     k_steps = all_reduce(mail, here, k_part, k_out, k_k, k_y, k_x, k_z, True)
     next(k_steps)
     x_core.wait_recv()
-    mail.settle([x_core])
 
     @pl.loop(0, 8)
     def _(i):
@@ -399,8 +428,6 @@
                 mail.send(r1.at[rows48(zl * 4 + (here.y + d) % 4)], r2.at[d - 1, zl], here.at(dy=d))
             )
     next(k_steps)
-    next(e_steps)
-    next(e_steps)
     next(e_steps)
 
     x_copies = {}
@@ -432,6 +459,63 @@
                     m[:, where, :] = lt[:, rows, :]
         return copies
 
+    for copy in t_x:
+        copy.wait_recv()
+    for zh in range(4):
+        where = target(zh, 0)
+        xt[where, :] = xt[where, :] + (q1[0, zh] + q1[1, zh])
+    t_z = [
+        mail.send(xt.at[rows48((here.zh + d) % 4 * 4 + here.x)], q2.at[d - 1], here.at(dz=2 * d))
+        for d in (1, 2, 3)
+    ]
+    for copy in x_y:
+        copy.wait_recv()
+    for zl in range(2):
+        where = rows48(zl * 4 + here.y)
+        r1[where, :] = r1[where, :] + (r2[0, zl] + r2[1, zl] + r2[2, zl])
+    x_z = mail.send(r1.at[rows48((1 - here.zl) * 4 + here.y)], r3, here.zl_peer())
+    along_x(0)
+    for d in (2, 6, 4, 1, 7, 3, 5):
+        z_copies[d].wait_recv()
+        along_x(d)
+    next(e_steps)
+    next(k_steps)
+    mail.settle(z_copies.values())
+    next(k_steps)
+    next(e_steps)
+    x_z.wait_recv()
+    for copy in t_z:
+        copy.wait_recv()
+    piece = r1[rows48(here.zl * 4 + here.y), :] + r3[...]
+    piece = 0.5 * (piece + xt[rows48(here.f), :] + (q2[0] + q2[1] + q2[2]))
+    xr, xc = uc, ur
+    xc[rows48(here.f), :] = piece
+    xr[rows48(here.slot), :] = piece
+    closing = list(mail.open)
+    row_steps, col_steps = gather_row(mail, here, xc, []), gather_col(mail, here, xr, [])
+    next(row_steps)
+    next(col_steps)
+    next(k_steps)
+    next(e_steps)
+    next(col_steps)
+    next(row_steps)
+    next(k_steps)
+    next(e_steps)
+    next(row_steps)
+    next(row_steps)
+    next(k_steps)
+    next(e_steps)
+    m_copies = []
+    for zl, deltas in ((here.zl, (0, 2, 6, 4)), (1 - here.zl, (1, 7, 3, 5))):
+        for d in deltas:
+            for copy in x_copies[d]:
+                copy.wait_recv()
+        m_copies += shuffle(zl)
+    next(row_steps)
+    next(col_steps)
+    next(col_steps)
+    next(e_steps)
+
     e = jnp.concatenate([e_out[:, :B], e_out[:, B:]], axis=0)
     for p, value in ((0, e), (1, e.T)):
         high, low = split(value)
@@ -447,62 +531,9 @@
     less(uch, bch)
     less(urh, brh)
 
-    along_x(0)
-    for d in (2, 6, 4):
-        z_copies[d].wait_recv()
-        along_x(d)
-    for copy in t_x:
-        copy.wait_recv()
-    for zh in range(4):
-        where = rows48(zh * 4 + here.x)
-        xt[where, :] = xt[where, :] + (q1[0, zh] + q1[1, zh] + q1[2, zh])
-    t_z = [
-        mail.send(xt.at[rows48((here.zh + d) % 4 * 4 + here.x)], q2.at[d - 1], here.at(dz=2 * d))
-        for d in (1, 2, 3)
-    ]
-    for copy in x_y:
-        copy.wait_recv()
-    for zl in range(2):
-        where = rows48(zl * 4 + here.y)
-        r1[where, :] = r1[where, :] + (r2[0, zl] + r2[1, zl] + r2[2, zl])
-    x_z = mail.send(r1.at[rows48((1 - here.zl) * 4 + here.y)], r3, here.zl_peer())
-    next(k_steps)
-    for d in (1, 7, 3, 5):
-        z_copies[d].wait_recv()
-        along_x(d)
-    mail.settle(z_copies.values())
-    for d in (0, 2, 6, 4):
-        for copy in x_copies[d]:
-            copy.wait_recv()
-    m_copies = shuffle(here.zl)
-    next(k_steps)
-    x_z.wait_recv()
-    for copy in t_z:
-        copy.wait_recv()
-    piece = r1[rows48(here.zl * 4 + here.y), :] + r3[...]
-    piece = 0.5 * (piece + xt[rows48(here.f), :] + (q2[0] + q2[1] + q2[2]))
-    xr, xc = uc, ur
-    xc[rows48(here.f), :] = piece
-    xr[rows48(here.slot), :] = piece
-    row_steps, col_steps = gather_row(mail, here, xc, []), gather_col(mail, here, xr, [])
-    next(row_steps)
-    next(col_steps)
-    next(k_steps)
-    next(k_steps)
-    next(col_steps)
-    next(k_steps)
-    next(row_steps)
-    next(row_steps)
-    next(row_steps)
-    for d in (1, 7, 3, 5):
-        for copy in x_copies[d]:
-            copy.wait_recv()
-    m_copies += shuffle(1 - here.zl)
-    next(col_steps)
-    next(col_steps)
-    next(k_steps)
-    next(k_steps)
-    mail.settle()
+    next(k_steps)
+    next(k_steps)
+    mail.settle(closing)
 
     @pl.loop(0, 32)
     def _(i):
@@ -599,9 +630,9 @@
             vmem(M, U), vmem(M, U), vmem(2, 2, B, B, dtype=BF16),
             *[vmem(2, M, U, dtype=BF16)] * 4, vmem(2, U, M, dtype=BF16), *[vmem(2, M, B, dtype=BF16)] * 2,
             *sums(256),
-            vmem(M, U), vmem(3, 4, W, U), vmem(3, W, U), vmem(M // 2, U), vmem(3, 2, W, U), vmem(W, U),
+            vmem(M, U), vmem(2, 4, W, B), vmem(2, 4, W, U), vmem(3, W, U), vmem(M // 2, U), vmem(3, 2, W, U), vmem(W, U),
             *sums(M),
-            pltpu.SemaphoreType.DMA((176,)), pltpu.SemaphoreType.DMA((176,)), pltpu.SemaphoreType.DMA((4,)),
+            pltpu.SemaphoreType.DMA((184,)), pltpu.SemaphoreType.DMA((184,)), pltpu.SemaphoreType.DMA((4,)),
         ],
         compiler_params=pltpu.CompilerParams(
             collective_id=0, has_side_effects=True, vmem_limit_bytes=63 << 20

time: 290 us -> 223 us (0.77); the launches traced: 284 us -> 222 us
  Pallas kernels: 280 us -> 218 us
    pallas_call x1, Pallas kernels: 280 us -> 218 us  [on_device(): pl.pallas_call(kernel, name='panels', out_shape=jax.ShapeDtypeStruct((M *...]
where the time goes in v3:
time: 223 us; the launch traced here: 222 us
  Pallas kernels  218 us (98%)
  local copies, waits for them, and re-layouts  4.69 us (2%)
    pallas_call x1, Pallas kernels, on_device(): pl.pallas_call(kernel, name='panels', out_shape=jax.ShapeDtypeStruct((M *...  218 us
    unnamed x1, local copies, waits for them, and re-layouts  4.69 us

profile of v3, /device:TPU:1, one launch (start us, length us, event | category | flops | bytes accessed | tf_op | source)
XLA Modules:
  0.0 222.4 jit_solution(13718050262679089764)
XLA Ops:
  0.0 217.7 %panels.1 = f32[4608,128]{1,0:T(8,128)} custom-call(f32[4608,128]{1,0:T(8,128)} %bitcast.4, f32[48,1024]{1,0:T(8,128)} %bitcast.5, f32[2,512,512]{2,1,0:T(8,128)} %t.1), custom_call_target="tpu_custom_call" | custom-call | tf_op jit(solution)/shard_map/panels/pallas_call | solution.py:622
  217.7 4.7 %copy.6 = f32[1,768,1,768]{3,2,1,0:T(1,128)} copy(f32[1,768,1,768]{3,2,1,0:T(1,128)} %bitcast.3) | data formatting | bytes 4718592

commit v4 on v3

--- a/solution.py
+++ b/solution.py
@@ -144,30 +144,49 @@
 def gather_col(mail, here, buf, log):
     send = logged(mail, log)
 
-    def block(zl):
-        return buf.at[rows48(here.slot_of(here.k, zl, here.y))]
-
-    mine = block(here.zl)
+    def block(zl, y):
+        return buf.at[rows48(here.slot_of(here.k, zl, y % NY))]
+
+    def half(zl, y, which):
+        return buf.at[rows48(here.slot_of(here.k, zl, y % NY)), pl.ds(which * B, B)]
+
+    def both(zl):
+        mine = block(zl, here.y)
+        return zl, send(mine, mine, here.at(dy=1)), send(mine, mine, here.at(dy=3))
+
+    def pass_on(zl, from_left, from_right):
+        from_left.wait_recv()
+        part = half(zl, here.y + 3, 0)
+        one = send(part, part, here.at(dy=1))
+        from_right.wait_recv()
+        part = half(zl, here.y + 1, 1)
+        return zl, one, send(part, part, here.at(dy=3))
+
+    def across(zl, one, two):
+        one.wait_recv()
+        two.wait_recv()
+        part = buf.at[pl.ds(pl.multiple_of((here.k * 8 + zl * 4) * W, 8), 4 * W)]
+        return send(part, part, here.at(dk=1))
+
+    mine = block(here.zl, here.y)
     pair = send(mine, mine, here.zl_peer())
-    first = [send(mine, mine, here.at(dy=d)) for d in (1, 2, 3)]
+    first = both(here.zl)
     yield
     pair.wait_recv()
-    got = block(1 - here.zl)
-    second = [send(got, got, here.at(dy=d)) for d in (1, 2, 3)]
-    yield
-    last = []
-    for zl, copies in ((here.zl, first), (1 - here.zl, second)):
-        for copy in copies:
-            copy.wait_recv()
-        part = buf.at[pl.ds(pl.multiple_of((here.k * 8 + zl * 4) * W, 8), 4 * W)]
-        last.append(send(part, part, here.at(dk=1)))
-        yield
-    for copy in last:
-        copy.wait_recv()
-    yield
-
-
-def all_reduce(mail, here, part, out, from_k, from_y, from_x, from_z, swap):
+    second = both(1 - here.zl)
+    first = pass_on(*first)
+    yield
+    second = pass_on(*second)
+    first = across(*first)
+    yield
+    second = across(*second)
+    yield
+    first.wait_recv()
+    second.wait_recv()
+    yield
+
+
+def all_reduce(mail, here, part, out, from_k, from_y, from_x, from_z):
     half = part.shape[0] // 2
     plane, block = half // 4, half // 16
 
@@ -231,9 +250,8 @@
     total = part[where, lanes(here.z)]
     for p in range(7):
         total = total + from_z[p * block : (p + 1) * block, :]
-    outer, inner = (here.x, here.y) if swap else (here.y, here.x)
-    base = (here.k * 4 + outer) * plane
-    where = rows(base + inner * block, block)
+    base = (here.k * 4 + here.y) * plane
+    where = rows(base + here.x * block, block)
     out[where, lanes(here.z)] = total
     mine = out.at[where, lanes(here.z)]
     copies = [mail.send(mine, mine, here.at(dz=d)) for d in range(1, 8)]
@@ -241,12 +259,12 @@
     for copy in copies:
         copy.wait_recv()
     mine = out.at[where]
-    copies = [mail.send(mine, mine, here.at(dy=d) if swap else here.at(dx=d)) for d in (1, 2, 3)]
+    copies = [mail.send(mine, mine, here.at(dx=d)) for d in (1, 2, 3)]
     yield
     for copy in copies:
         copy.wait_recv()
     mine = out.at[rows(base, plane)]
-    copies = [mail.send(mine, mine, here.at(dx=d) if swap else here.at(dy=d)) for d in (1, 2, 3)]
+    copies = [mail.send(mine, mine, here.at(dy=d)) for d in (1, 2, 3)]
     yield
     for copy in copies:
         copy.wait_recv()
@@ -303,7 +321,7 @@
     part = mm(split(u[:, :B].T), own_second)
     e_part[:, :B] = part[:256]
     e_part[:, B:] = part[256:]
-    e_steps = all_reduce(mail, here, e_part, e_out, e_k, e_y, e_x, e_z, False)
+    e_steps = all_reduce(mail, here, e_part, e_out, e_k, e_y, e_x, e_z)
     next(e_steps)
     next(col_steps)
 
@@ -413,7 +431,7 @@
             k_part[B:, 256 * c : 256 * c + 256] = value[:256]
             k_part[B:, where] = value[256:]
     mail.settle([x_core])
-    k_steps = all_reduce(mail, here, k_part, k_out, k_k, k_y, k_x, k_z, True)
+    k_steps = all_reduce(mail, here, k_part, k_out, k_k, k_y, k_x, k_z)
     next(k_steps)
     x_core.wait_recv()
 
@@ -531,16 +549,38 @@
     less(uch, bch)
     less(urh, brh)
 
-    next(k_steps)
+    def add_to_tile(j, scale, value):
+        for slot in range(16):
+            tile_row = slot // 4 % 2 * 8 + slot % 4 * 2 + slot // 8
+            for e in range(2):
+                where = pl.ds(tile_row * (6 * W) + j * 2 + e, W, stride=6)
+                hb[where, :] = scale * hb[where, :] - value[slot * W : (slot + 1) * W, 128 * e : 128 * e + 128]
+
+    next(col_steps)
+    next(row_steps)
+
+    @pl.loop(0, 3)
+    def _(i):
+        put(p0, (columns(i), EVERY), xr[columns(i), :])
+        put(p1, (columns(i), EVERY), xc[columns(i), :])
+
+    next(k_steps)
+
+    @pl.loop(0, 3)
+    def _(j):
+        rows = columns(j)
+        value = mm(hl(p0, EVERY, ONE), hl(bch, rows, EVERY), NT)
+        value = value + mm(hl(p0, EVERY, TWO), hl(uch, rows, TWO), NT)
+        value = value + mm(hl(brh, EVERY, EVERY), hl(p1, rows, ONE), NT)
+        value = value + mm(hl(urh, EVERY, TWO), hl(p1, rows, TWO), NT)
+        add_to_tile(j, 0.5, value)
+
     next(k_steps)
     mail.settle(closing)
 
-    @pl.loop(0, 32)
+    @pl.loop(0, 3)
     def _(i):
-        k, y, x = i // 16, i // 4 % 4, i % 4
-        k_part[pl.ds(pl.multiple_of(i * 24, 8), 24), :] = k_out[
-            pl.ds(pl.multiple_of((k * 16 + x * 4 + y) * 24, 8), 24), :
-        ]
+        k_part[columns(i), :] = k_out[columns(i), :]
 
     k_part[:B, :B] = 0.5 * (k_part[:B, :B] + k_part[:B, :B].T)
 
@@ -564,33 +604,9 @@
         rows = xt[256 * i : 256 * i + 256, :] if i < 3 else e_part[...]
         put(p2, (slice(256 * i, 256 * i + 256), EVERY), mm(split(rows), hl(uch, EVERY, EVERY), NT))
 
-    def add_to_tile(j, scale, value):
-        for slot in range(16):
-            tile_row = slot // 4 % 2 * 8 + slot % 4 * 2 + slot // 8
-            for e in range(2):
-                where = pl.ds(tile_row * (6 * W) + j * 2 + e, W, stride=6)
-                hb[where, :] = scale * hb[where, :] - value[slot * W : (slot + 1) * W, 128 * e : 128 * e + 128]
-
     @pl.loop(0, 3)
     def _(j):
-        add_to_tile(j, 0.5, mm(hl(urh, EVERY, EVERY), hl(p2, EVERY, columns(j))))
-
-    next(col_steps)
-    next(row_steps)
-
-    @pl.loop(0, 3)
-    def _(i):
-        put(p0, (columns(i), EVERY), xr[columns(i), :])
-        put(p1, (columns(i), EVERY), xc[columns(i), :])
-
-    @pl.loop(0, 3)
-    def _(j):
-        rows = columns(j)
-        value = mm(hl(p0, EVERY, ONE), hl(bch, rows, EVERY), NT)
-        value = value + mm(hl(p0, EVERY, TWO), hl(uch, rows, TWO), NT)
-        value = value + mm(hl(brh, EVERY, EVERY), hl(p1, rows, ONE), NT)
-        value = value + mm(hl(urh, EVERY, TWO), hl(p1, rows, TWO), NT)
-        add_to_tile(j, 1.0, value)
+        add_to_tile(j, 1.0, mm(hl(urh, EVERY, EVERY), hl(p2, EVERY, columns(j))))
 
     for copy in m_copies:
         copy.wait_recv()
@@ -632,7 +648,7 @@
             *sums(256),
             vmem(M, U), vmem(2, 4, W, B), vmem(2, 4, W, U), vmem(3, W, U), vmem(M // 2, U), vmem(3, 2, W, U), vmem(W, U),
             *sums(M),
-            pltpu.SemaphoreType.DMA((184,)), pltpu.SemaphoreType.DMA((184,)), pltpu.SemaphoreType.DMA((4,)),
+            pltpu.SemaphoreType.DMA((192,)), pltpu.SemaphoreType.DMA((192,)), pltpu.SemaphoreType.DMA((4,)),
         ],
         compiler_params=pltpu.CompilerParams(
             collective_id=0, has_side_effects=True, vmem_limit_bytes=63 << 20

time: 223 us -> 245 us (1.099)
  Pallas kernels: 218 us -> 238 us
    pallas_call x1, Pallas kernels: 218 us -> 238 us  [on_device(): pl.pallas_call(kernel, name='panels', out_shape=jax.ShapeDtypeStruct((M *...]
where the time goes in v4:
time: 245 us; the launch traced here: 243 us
  Pallas kernels  238 us (97%)
  local copies, waits for them, and re-layouts  4.69 us (2%)
    pallas_call x1, Pallas kernels, on_device(): pl.pallas_call(kernel, name='panels', out_shape=jax.ShapeDtypeStruct((M *...  238 us

profile of v4, /device:TPU:1, one launch (start us, length us, event | category | flops | bytes accessed | tf_op | source)
XLA Modules:
  0.0 243.2 jit_solution(7382327308872869647)
XLA Ops:
  0.0 238.5 %panels.1 = f32[4608,128]{1,0:T(8,128)} custom-call(f32[4608,128]{1,0:T(8,128)} %bitcast.4, f32[48,1024]{1,0:T(8,128)} %bitcast.5, f32[2,512,512]{2,1,0:T(8,128)} %t.1), custom_call_target="tpu_custom_call" | custom-call | tf_op jit(solution)/shard_map/panels/pallas_call | solution.py:638
  238.5 4.7 %copy.6 = f32[1,768,1,768]{3,2,1,0:T(1,128)} copy(f32[1,768,1,768]{3,2,1,0:T(1,128)} %bitcast.3) | data formatting | bytes 4718592

commit v5 on v3

--- a/solution.py
+++ b/solution.py
@@ -531,7 +531,32 @@
     less(uch, bch)
     less(urh, brh)
 
-    next(k_steps)
+    def add_to_tile(j, scale, value):
+        for slot in range(16):
+            tile_row = slot // 4 % 2 * 8 + slot % 4 * 2 + slot // 8
+            for e in range(2):
+                where = pl.ds(tile_row * (6 * W) + j * 2 + e, W, stride=6)
+                hb[where, :] = scale * hb[where, :] - value[slot * W : (slot + 1) * W, 128 * e : 128 * e + 128]
+
+    next(col_steps)
+    next(row_steps)
+
+    @pl.loop(0, 3)
+    def _(i):
+        put(p0, (columns(i), EVERY), xr[columns(i), :])
+        put(p1, (columns(i), EVERY), xc[columns(i), :])
+
+    next(k_steps)
+
+    @pl.loop(0, 3)
+    def _(j):
+        rows = columns(j)
+        value = mm(hl(p0, EVERY, ONE), hl(bch, rows, EVERY), NT)
+        value = value + mm(hl(p0, EVERY, TWO), hl(uch, rows, TWO), NT)
+        value = value + mm(hl(brh, EVERY, EVERY), hl(p1, rows, ONE), NT)
+        value = value + mm(hl(urh, EVERY, TWO), hl(p1, rows, TWO), NT)
+        add_to_tile(j, 0.5, value)
+
     next(k_steps)
     mail.settle(closing)
 
@@ -564,33 +589,9 @@
         rows = xt[256 * i : 256 * i + 256, :] if i < 3 else e_part[...]
         put(p2, (slice(256 * i, 256 * i + 256), EVERY), mm(split(rows), hl(uch, EVERY, EVERY), NT))
 
-    def add_to_tile(j, scale, value):
-        for slot in range(16):
-            tile_row = slot // 4 % 2 * 8 + slot % 4 * 2 + slot // 8
-            for e in range(2):
-                where = pl.ds(tile_row * (6 * W) + j * 2 + e, W, stride=6)
-                hb[where, :] = scale * hb[where, :] - value[slot * W : (slot + 1) * W, 128 * e : 128 * e + 128]
-
     @pl.loop(0, 3)
     def _(j):
-        add_to_tile(j, 0.5, mm(hl(urh, EVERY, EVERY), hl(p2, EVERY, columns(j))))
-
-    next(col_steps)
-    next(row_steps)
-
-    @pl.loop(0, 3)
-    def _(i):
-        put(p0, (columns(i), EVERY), xr[columns(i), :])
-        put(p1, (columns(i), EVERY), xc[columns(i), :])
-
-    @pl.loop(0, 3)
-    def _(j):
-        rows = columns(j)
-        value = mm(hl(p0, EVERY, ONE), hl(bch, rows, EVERY), NT)
-        value = value + mm(hl(p0, EVERY, TWO), hl(uch, rows, TWO), NT)
-        value = value + mm(hl(brh, EVERY, EVERY), hl(p1, rows, ONE), NT)
-        value = value + mm(hl(urh, EVERY, TWO), hl(p1, rows, TWO), NT)
-        add_to_tile(j, 1.0, value)
+        add_to_tile(j, 1.0, mm(hl(urh, EVERY, EVERY), hl(p2, EVERY, columns(j))))
 
     for copy in m_copies:
         copy.wait_recv()

time: 223 us -> 219 us (0.982)
  Pallas kernels: 218 us -> 214 us
    pallas_call x1, Pallas kernels: 218 us -> 214 us  [on_device(): pl.pallas_call(kernel, name='panels', out_shape=jax.ShapeDtypeStruct((M *...]
where the time goes in v5:
time: 219 us; the launch traced here: 218 us
  Pallas kernels  214 us (98%)
  local copies, waits for them, and re-layouts  4.69 us (2%)
    pallas_call x1, Pallas kernels, on_device(): pl.pallas_call(kernel, name='panels', out_shape=jax.ShapeDtypeStruct((M *...  214 us
    unnamed x1, local copies, waits for them, and re-layouts  4.69 us

profile of v5, /device:TPU:1, one launch (start us, length us, event | category | flops | bytes accessed | tf_op | source)
XLA Modules:
  0.0 218.4 jit_solution(1777404471255334124)
XLA Ops:
  0.0 213.7 %panels.1 = f32[4608,128]{1,0:T(8,128)} custom-call(f32[4608,128]{1,0:T(8,128)} %bitcast.4, f32[48,1024]{1,0:T(8,128)} %bitcast.5, f32[2,512,512]{2,1,0:T(8,128)} %t.1), custom_call_target="tpu_custom_call" | custom-call | tf_op jit(solution)/shard_map/panels/pallas_call | solution.py:623
  213.7 4.7 %copy.6 = f32[1,768,1,768]{3,2,1,0:T(1,128)} copy(f32[1,768,1,768]{3,2,1,0:T(1,128)} %bitcast.3) | data formatting | bytes 4718592
